TPU v7x, 512 devices: a whole 4x4x16 slice. The times are simulated.
512 devices in a mesh: tensor: 16 (over x, z_hi), feature: 8 (over y, core), dp: 4 (over z_lo).
Axes of the slice: x: 4, y: 4, z: 16 (z_hi: 4, z_lo: 4; z = z_hi * 4 + z_lo), core: 2. Of those that a mesh axis runs over, the one named last changes fastest.
Arguments:
- mlp_input: bfloat16 [64, 4096], P(None, ('feature', 'dp')), may hold values from -6 to 6
- gate_weight: bfloat16 [4096, 28672], P(('feature', 'dp'), 'tensor'), may hold values from -0.09375 to 0.09375
- up_weight: bfloat16 [4096, 28672], P(('feature', 'dp'), 'tensor'), may hold values from -0.09375 to 0.09375
- down_weight: bfloat16 [28672, 4096], P('tensor', ('feature', 'dp')), may hold values from -0.03125 to 0.03125
- down_encoder: bfloat16 [65536, 4096], P('tensor', ('feature', 'dp')), may hold values from -6 to 6
- feature_ids: int32 [32], replicated, may hold values from 0 to 65535
- up_decoder: bfloat16 [131072, 4096], P('tensor', ('feature', 'dp')), may hold values from -0.09375 to 0.09375
- latent_ids: int32 [64, 64], replicated, may hold values from 0 to 131071, as said below
- latent_acts: float32 [64, 64], P('dp', 'tensor'), may hold values from 0.5 to 4
Outputs:
- attribution: float32 [32, 64, 64], P('feature', 'dp', 'tensor')
Inputs may be any that keep to these rules, and one draw needn't show every extreme that they name: `latent_ids`: the 64 latents of one token are distinct.
All inputs are finite; a program needn't handle non-finite values.
Results may differ from a plain program's by a relative error of at most 0.0029.
Values may be sent and summed in bfloat16 or wider, within the bound.
No kernel may reach another device: no remote copies, remote signals or barrier semaphores. Data moves between devices by JAX's collectives and lax.ppermute only.
A program may use at most 64 MiB of HBM per device.

v0:
```python
import math
import jax
import jax.numpy as jnp
from jax import lax
from jax.sharding import PartitionSpec as P


def factors(gate_pre, up_pre):
    sigmoid_gate = jax.nn.sigmoid(gate_pre)
    gate_factor = up_pre * sigmoid_gate * (1.0 + gate_pre * (1.0 - sigmoid_gate))
    up_factor = gate_pre * sigmoid_gate
    return (gate_factor, up_factor)


def arrange_blocks(partial_value, count_tensor, count_feature, count_data):
    features = partial_value.shape[0]
    tokens = partial_value.shape[1]
    slots = partial_value.shape[2]
    arranged = partial_value.reshape(
        count_feature,
        features // count_feature,
        count_data,
        tokens // count_data,
        count_tensor,
        slots // count_tensor,
    )
    arranged = arranged.transpose(4, 0, 2, 1, 3, 5)
    return arranged.reshape(
        count_tensor * count_feature * count_data,
        features // count_feature,
        tokens // count_data,
        slots // count_tensor,
    )


def on_device(
    mlp_input,
    gate_weight,
    up_weight,
    down_weight,
    down_encoder,
    feature_ids,
    up_decoder,
    latent_ids,
    latent_acts,
):
    contract = (((1,), (1,)), ((), ()))
    tensor_rank = lax.axis_index("tensor")
    tokens = mlp_input.shape[0]
    dblk = gate_weight.shape[0]
    ffblk = gate_weight.shape[1]
    features = feature_ids.shape[0]
    count_tensor = lax.axis_size("tensor")
    count_feature = lax.axis_size("feature")
    count_data = lax.axis_size("dp")
    enc_rows = down_encoder.shape[0]
    local_ids = feature_ids - tensor_rank * enc_rows
    picker = (local_ids[:, None] == jnp.arange(enc_rows, dtype=jnp.int32)[None, :]).astype(
        jnp.bfloat16
    )
    chosen = lax.psum(jnp.dot(picker, down_encoder, preferred_element_type=jnp.float32), "tensor")
    cotangent = chosen.astype(jnp.bfloat16)
    neuron_part = lax.dot_general(
        cotangent, down_weight, contract, preferred_element_type=jnp.float32
    )
    gate_part = jnp.dot(mlp_input, gate_weight, preferred_element_type=jnp.float32)
    up_part = jnp.dot(mlp_input, up_weight, preferred_element_type=jnp.float32)
    gate_pre, up_pre, neuron_grad = lax.psum((gate_part, up_part, neuron_part), ("feature", "dp"))
    gate_factor, up_factor = factors(gate_pre, up_pre)
    per_block = math.gcd(features, 8)
    grouped_rows = neuron_grad.reshape(features // per_block, per_block, ffblk)

    def feature_block(grad_rows):
        grad_gate = (
            (grad_rows[:, None, :] * gate_factor[None])
            .astype(jnp.bfloat16)
            .reshape(per_block * tokens, ffblk)
        )
        grad_up = (
            (grad_rows[:, None, :] * up_factor[None])
            .astype(jnp.bfloat16)
            .reshape(per_block * tokens, ffblk)
        )
        width_grad = lax.dot_general(
            grad_gate, gate_weight, contract, preferred_element_type=jnp.float32
        )
        width_grad = width_grad + lax.dot_general(
            grad_up, up_weight, contract, preferred_element_type=jnp.float32
        )
        return width_grad.reshape(per_block, tokens, dblk)

    width_part = lax.map(feature_block, grouped_rows).reshape(features, tokens, dblk)
    dec_rows = up_decoder.shape[0]
    local_latents = latent_ids - tensor_rank * dec_rows
    owner_mask = jnp.logical_and(local_latents >= 0, local_latents < dec_rows)
    picked = jnp.take(up_decoder, jnp.clip(local_latents, 0, dec_rows - 1), axis=0)
    picked = picked * owner_mask[:, :, None].astype(jnp.bfloat16)
    width_full = lax.psum(width_part, "tensor")
    partial_value = jnp.einsum(
        "ftd,tkd->ftk", width_full, picked.astype(jnp.float32), precision=lax.Precision.HIGHEST
    )
    arranged = arrange_blocks(partial_value, count_tensor, count_feature, count_data)
    own_block = lax.psum_scatter(
        arranged, ("tensor", "feature", "dp"), scatter_dimension=0, tiled=True
    )[0]
    return own_block * latent_acts[None, :, :]


def solution(mesh):
    in_specs = (
        P(None, ("feature", "dp")),
        P(("feature", "dp"), "tensor"),
        P(("feature", "dp"), "tensor"),
        P("tensor", ("feature", "dp")),
        P("tensor", ("feature", "dp")),
        P(),
        P("tensor", ("feature", "dp")),
        P(),
        P("dp", "tensor"),
    )
    out_specs = P("feature", "dp", "tensor")
    return jax.shard_map(
        on_device, mesh=mesh, in_specs=in_specs, out_specs=out_specs, check_vma=False
    )
```

profile of v0, /device:TPU:2, one launch (start us, length us, event | category | flops | bytes accessed | tf_op | source)
XLA Modules:
  0.0 1137.1 jit_solution(10292003025647488974)
XLA Ops:
  6.5 0.0 copy-start
  6.5 0.0 copy-start.1
  6.5 0.0 copy-start.3
  6.5 0.0 all-reduce.10.cloned.1.call-start
  6.6 0.8 broadcast_subtract_fusion
  7.4 1.6 fusion.5
  9.0 99.8 %psum.35 = bf16[32,128]{1,0:T(8,128)(2,1)S(1)} all-reduce(f32[32,128]{1,0:T(8,128)S(1)} %fusion.5), channel_id=1, replica_groups=mesh['tensor'=16,'feature'=8,'dp'=4] {'tensor'}, use_global_device_ids=true, to_apply=%region_0.0 | all-reduce | flops 4096 | bytes 24576 | tf_op jit(solution)/shard_map/psum | solution.py:61
  108.8 2.0 fusion.12
  110.8 0.0 copy-done.1
  110.8 1.7 fusion.13
  112.5 0.0 copy-done.3
  112.5 1.0 convolution_bitcast_fusion
  113.5 0.0 all-reduce.10.cloned.1.call-update
  113.5 0.0 all-reduce.6.cloned.1.call-start
  113.5 283.3 %all-reduce.10.cloned.1.call-done = (f32[4,8,1792]{2,1,0:T(8,128)}, f32[64,1792]{1,0:T(8,128)}, f32[64,1792]{1,0:T(8,128)}) async-done(((f32[4,8,1792]{2,1,0:T(8,128)}, f32[64,1792]{1,0:T(8,128)}, f32[64,1792]{1,0:T(8,128)}), (f32[4,8,1792]{2,1,0:T(8,128)}, f32[64,1792]{1,0:T(8,128)}, f32[64,1792]{1,0:T(8,128)})) %all-reduce.10.cloned.1.call-update) | async-done | bytes 1146896 | tf_op jit(solution)/shard_map/psum | solution.py:68
  396.9 1.4 fusion.6
  398.2 0.0 copy-start.4
  398.2 16.5 %while.10 = (s32[]{:T(128)}, f32[4,8,64,128]{3,1,0,2:T(8,128)}, f32[4,8,1792]{2,1,0:T(8,128)}, f32[64,1792]{1,0:T(8,128)S(1)}, bf16[128,1792]{1,0:T(8,128)(2,1)S...) while((s32[]{:T(128)}, f32[4,8,64,128]{3,1,0,2:T(8,128)}, f32[4,8,1792]{2,1,0:T(8,128)}, ...), condition=%wide.region_5.6_spmd, body=%wide.region_4.5_spmd.sunk | while | flops 473497600 | bytes 12493429 | solution.py:92
  398.3 0.8 dynamic-slice_bitcast_fusion.3
  399.1 0.7 multiply_convert_fusion.3
  399.8 0.0 copy-start.2
  399.8 0.6 fusion.35
  400.5 0.4 copy-done.2
  400.8 0.6 convolution_add_fusion.2
  401.5 0.9 copy_dynamic-update-slice_fusion.2
  402.4 0.8 dynamic-slice_bitcast_fusion.3
  403.2 0.7 multiply_convert_fusion.3
  403.9 0.0 copy-start.2
  403.9 0.6 fusion.35
  404.6 0.4 copy-done.2
  404.9 0.6 convolution_add_fusion.2
  405.6 0.9 copy_dynamic-update-slice_fusion.2
  406.5 0.8 dynamic-slice_bitcast_fusion.3
  407.3 0.7 multiply_convert_fusion.3
  408.0 0.0 copy-start.2
  408.0 0.6 fusion.35
  408.7 0.4 copy-done.2
  409.0 0.6 convolution_add_fusion.2
  409.7 0.9 copy_dynamic-update-slice_fusion.2
  410.6 0.8 dynamic-slice_bitcast_fusion.3
  411.5 0.7 multiply_convert_fusion.3
  412.2 0.0 copy-start.2
  412.2 0.6 fusion.35
  412.8 0.4 copy-done.2
  413.2 0.6 convolution_add_fusion.2
  413.9 0.9 copy_dynamic-update-slice_fusion.2
  414.8 0.0 all-reduce.6.cloned.1.call-update
  414.8 0.0 all-reduce.8.cloned.1.call-start
  414.8 0.0 copy-done.4
  414.9 0.1 reshape.43
  415.0 0.0 copy-done
  415.0 12.1 %gather_fusion = bf16[4096,128]{1,0:T(8,128)(2,1)S(1)} fusion(bf16[8192,128]{1,0:T(8,128)(2,1)S(1)} %copy-done, s32[4096]{0:T(1024)S(1)} %broadcast_clamp_fusion), kind=kCustom, calls=%fused_computation | custom fusion | bytes 2113536 | tf_op jit(solution)/shard_map/jit(_take)/gather | solution.py:96
  427.1 197.9 %all-reduce.6.cloned.1.call-done = f32[32,64,128]{2,0,1:T(8,128)} async-done(((f32[32,64,128]{2,0,1:T(8,128)}), f32[32,64,128]{2,0,1:T(8,128)}) %all-reduce.6.cloned.1.call-update) | async-done | bytes 1048592 | tf_op jit(solution)/shard_map/psum | solution.py:98
  625.0 4.4 convolution_bitcast_fusion.1
  629.3 1.8 copy.18
  631.1 3.2 reshape.39
  634.3 3.4 copy.19
  637.7 4.7 copy.20
  642.4 0.0 copy-start.5
  642.4 0.0 all-reduce.8.cloned.1.call-update
  642.4 486.8 %all-reduce.8.cloned.1.call-done = f32[512,4,16,4]{2,3,1,0:T(4,128)} async-done(((f32[512,4,16,4]{2,3,1,0:T(4,128)}), f32[512,4,16,4]{2,3,1,0:T(4,128)}) %all-reduce.8.cloned.1.call-update) | async-done | bytes 524304
  1129.2 0.0 copy-done.5
  1129.2 1.3 fusion.8
  (3 shorter events, 0.0 us)
Async XLA Ops:
  6.5 408.4 %copy-start = (bf16[8192,128]{1,0:T(8,128)(2,1)S(1)}, bf16[8192,128]{1,0:T(8,128)(2,1)}, u32[]{:S(2)}) copy-start(bf16[8192,128]{1,0:T(8,128)(2,1)} %param.17) | copy-start | bytes 6291460
  6.5 104.3 %copy-start.1 = (bf16[128,1792]{1,0:T(8,128)(2,1)S(1)}, bf16[128,1792]{1,0:T(8,128)(2,1)}, u32[]{:S(2)}) copy-start(bf16[128,1792]{1,0:T(8,128)(2,1)} %param.12) | copy-start | bytes 1376260
  6.5 106.0 %copy-start.3 = (bf16[1792,128]{1,0:T(8,128)(2,1)S(1)}, bf16[1792,128]{1,0:T(8,128)(2,1)}, u32[]{:S(2)}) copy-start(bf16[1792,128]{1,0:T(8,128)(2,1)} %param.14) | copy-start | bytes 1376260
  6.5 390.3 %all-reduce.10.cloned.1.call-start = ((), (), s32[]{:S(2)}) async-start(), calls=%async_computation.2 | async-start | bytes 2293760 | tf_op jit(solution)/shard_map/psum | solution.py:68
  113.5 511.5 %all-reduce.6.cloned.1.call-start = ((), (), s32[]{:S(2)}) async-start(), calls=%async_computation | async-start | bytes 2097152 | tf_op jit(solution)/shard_map/psum | solution.py:98
  398.2 16.6 %copy-start.4 = (s32[64,64]{1,0:T(8,128)S(1)}, s32[64,64]{1,0:T(8,128)}, u32[]{:S(2)}) copy-start(s32[64,64]{1,0:T(8,128)} %param.18) | copy-start | bytes 49156
  399.8 1.0 copy-start.2
  403.9 1.0 copy-start.2
  408.0 1.0 copy-start.2
  412.2 1.0 copy-start.2
  414.8 714.4 %all-reduce.8.cloned.1.call-start = ((), (), s32[]{:S(2)}) async-start(), calls=%async_computation.1 | async-start | bytes 8388608
  642.4 486.9 %copy-start.5 = (f32[16,4]{0,1:T(4,128)S(1)}, f32[16,4]{0,1:T(4,128)}, u32[]{:S(2)}) copy-start(f32[16,4]{0,1:T(4,128)} %param.19) | copy-start | bytes 772
Sparse Core Ops, SparseCore 0:
  113.6 283.2 all-reduce.9
  414.9 210.0 all-reduce.5
  642.5 486.6 all-reduce.7
where the time goes:
time: 1140 us
  waiting for transfers between devices  968 us (85%)
  blocking collectives  99.8 us (9%)
  local copies, waits for them, and re-layouts  33.6 us (3%)
  matrix products  15.8 us (1%)
  between operations  13.2 us (1%)
    unnamed x4, waiting for transfers between devices  487 us
    psum x1, waiting for transfers between devices, on_device(): lax.psum((gate_part, up_part, neuron_part), ('feature', 'dp'))  283 us
    psum x1, waiting for transfers between devices, on_device(): width_full = lax.psum(width_part, 'tensor')  198 us
    psum x1, blocking collectives, on_device(): lax.psum(jnp.dot(picker, down_encoder, preferred_element_type=jnp.float32...  99.8 us
  transfers between devices with their start and end apart: 3, of which 3 were waited for; matrix products, arithmetic and copies ran while one was open for 1% of the time, Pallas kernels for 0%

commit v1 on v0

--- a/solution.py
+++ b/solution.py
@@ -44,6 +44,12 @@
     latent_ids,
     latent_acts,
 ):
+
+    def _number_slot(values):
+        after = lax.psum(values, "feature")
+        out_arr = lax.psum(after, "dp")
+        return out_arr
+
     contract = (((1,), (1,)), ((), ()))
     tensor_rank = lax.axis_index("tensor")
     tokens = mlp_input.shape[0]
@@ -65,7 +71,7 @@
     )
     gate_part = jnp.dot(mlp_input, gate_weight, preferred_element_type=jnp.float32)
     up_part = jnp.dot(mlp_input, up_weight, preferred_element_type=jnp.float32)
-    gate_pre, up_pre, neuron_grad = lax.psum((gate_part, up_part, neuron_part), ("feature", "dp"))
+    gate_pre, up_pre, neuron_grad = _number_slot((gate_part, up_part, neuron_part))
     gate_factor, up_factor = factors(gate_pre, up_pre)
     per_block = math.gcd(features, 8)
     grouped_rows = neuron_grad.reshape(features // per_block, per_block, ffblk)

time: 1140 us -> 1010 us (0.89)
  waiting for transfers between devices: 968 us -> 840 us
    psum x1 -> x2, waiting for transfers between devices: 283 us -> 155 us  [the longest x1 80.5 us: _number_slot(): out_arr = lax.psum(after, 'dp')]
    unnamed x4 -> x5, waiting for transfers between devices: 487 us -> 487 us
  transfers between devices with their start and end apart: 3 -> 4, of which waited for: 3 -> 4; matrix products, arithmetic and copies ran while one was open for 1% -> 1% of each run, Pallas kernels for 0% -> 0%
where the time goes in v1:
time: 1010 us
  waiting for transfers between devices  840 us (83%)
  blocking collectives  99.8 us (10%)
  local copies, waits for them, and re-layouts  33.6 us (3%)
  matrix products  15.8 us (2%)
  between operations  13.2 us (1%)
    unnamed x5, waiting for transfers between devices  487 us
    psum x1, waiting for transfers between devices, on_device(): width_full = lax.psum(width_part, 'tensor')  198 us
    psum x1, blocking collectives, on_device(): lax.psum(jnp.dot(picker, down_encoder, preferred_element_type=jnp.float32...  99.8 us
    psum x1, waiting for transfers between devices, _number_slot(): out_arr = lax.psum(after, 'dp')  80.5 us
    psum x1, waiting for transfers between devices, _number_slot(): after = lax.psum(values, 'feature')  74.3 us
  transfers between devices with their start and end apart: 4, of which 4 were waited for; matrix products, arithmetic and copies ran while one was open for 1% of the time, Pallas kernels for 0%

profile of v1, /device:TPU:2, one launch (start us, length us, event | category | flops | bytes accessed | tf_op | source)
XLA Modules:
  0.0 1008.8 jit_solution(5538792770304123222)
XLA Ops:
  6.5 0.0 copy-start
  6.5 0.0 copy-start.1
  6.5 0.0 all-reduce.12.cloned.1.call-start
  6.6 0.8 broadcast_subtract_fusion
  7.4 1.6 fusion.5
  9.0 99.8 %psum.56 = bf16[32,128]{1,0:T(8,128)(2,1)S(1)} all-reduce(f32[32,128]{1,0:T(8,128)S(1)} %fusion.5), channel_id=1, replica_groups=mesh['tensor'=16,'feature'=8,'dp'=4] {'tensor'}, use_global_device_ids=true, to_apply=%region_0.0 | all-reduce | flops 4096 | bytes 24576 | tf_op jit(solution)/shard_map/psum | solution.py:67
  108.8 2.0 fusion.13
  110.8 0.0 copy-done.1
  110.8 1.7 fusion.14
  112.5 0.0 copy-done.3
  112.5 1.0 fusion.15
  113.5 0.0 all-reduce.12.cloned.1.call-update
  113.5 0.0 all-reduce.14.cloned.1.call-start
  113.5 74.3 %all-reduce.12.cloned.1.call-done = (f32[32,1792]{1,0:T(8,128)}, f32[64,1792]{1,0:T(8,128)}, f32[64,1792]{1,0:T(8,128)}) async-done(((f32[32,1792]{1,0:T(8,128)}, f32[64,1792]{1,0:T(8,128)}, f32[64,1792]{1,0:T(8,128)}), (f32[32,1792]{1,0:T(8,128)}, f32[64,1792]{1,0:T(8,128)}, f32[64,1792]{1,0:T(8,128)})) %all-reduce.12.cloned.1.call-update) | async-done | bytes 1146896 | tf_op jit(solution)/shard_map/psum | solution.py:49
  187.8 0.0 all-reduce.14.cloned.1.call-update
  187.9 0.0 all-reduce.8.cloned.1.call-start
  187.9 80.5 %all-reduce.14.cloned.1.call-done = (f32[4,8,1792]{2,1,0:T(8,128)}, f32[64,1792]{1,0:T(8,128)}, f32[64,1792]{1,0:T(8,128)}) async-done(((f32[4,8,1792]{2,1,0:T(8,128)}, f32[64,1792]{1,0:T(8,128)}, f32[64,1792]{1,0:T(8,128)}), (f32[4,8,1792]{2,1,0:T(8,128)}, f32[64,1792]{1,0:T(8,128)}, f32[64,1792]{1,0:T(8,128)})) %all-reduce.14.cloned.1.call-update) | async-done | bytes 1146896 | tf_op jit(solution)/shard_map/psum | solution.py:50
  268.4 1.4 fusion.6
  269.8 0.0 copy-start.4
  269.8 16.5 %while.10 = (s32[]{:T(128)}, f32[4,8,64,128]{3,1,0,2:T(8,128)}, f32[4,8,1792]{2,1,0:T(8,128)}, f32[64,1792]{1,0:T(8,128)S(1)}, bf16[128,1792]{1,0:T(8,128)(2,1)S...) while((s32[]{:T(128)}, f32[4,8,64,128]{3,1,0,2:T(8,128)}, f32[4,8,1792]{2,1,0:T(8,128)}, ...), condition=%wide.region_8.9_spmd, body=%wide.region_7.8_spmd.sunk | while | flops 473497600 | bytes 12493429 | solution.py:98
  269.8 0.8 dynamic-slice_bitcast_fusion.3
  270.7 0.7 multiply_convert_fusion.3
  271.4 0.0 copy-start.2
  271.4 0.6 fusion.37
  272.0 0.4 copy-done.2
  272.4 0.6 convolution_add_fusion.2
  273.1 0.9 copy_dynamic-update-slice_fusion.2
  273.9 0.8 dynamic-slice_bitcast_fusion.3
  274.8 0.7 multiply_convert_fusion.3
  275.5 0.0 copy-start.2
  275.5 0.6 fusion.37
  276.1 0.4 copy-done.2
  276.5 0.6 convolution_add_fusion.2
  277.2 0.9 copy_dynamic-update-slice_fusion.2
  278.0 0.8 dynamic-slice_bitcast_fusion.3
  278.9 0.7 multiply_convert_fusion.3
  279.6 0.0 copy-start.2
  279.6 0.6 fusion.37
  280.3 0.4 copy-done.2
  280.6 0.6 convolution_add_fusion.2
  281.3 0.9 copy_dynamic-update-slice_fusion.2
  282.2 0.8 dynamic-slice_bitcast_fusion.3
  283.0 0.7 multiply_convert_fusion.3
  283.8 0.0 copy-start.2
  283.8 0.6 fusion.37
  284.4 0.4 copy-done.2
  284.8 0.6 convolution_add_fusion.2
  285.4 0.9 copy_dynamic-update-slice_fusion.2
  286.3 0.0 all-reduce.8.cloned.1.call-update
  286.3 0.0 all-reduce.10.cloned.1.call-start
  286.4 0.0 copy-done.4
  286.4 0.1 reshape.43
  286.5 0.0 copy-done
  286.5 12.1 %gather_fusion = bf16[4096,128]{1,0:T(8,128)(2,1)S(1)} fusion(bf16[8192,128]{1,0:T(8,128)(2,1)S(1)} %copy-done, s32[4096]{0:T(1024)S(1)} %broadcast_clamp_fusion), kind=kCustom, calls=%fused_computation | custom fusion | bytes 2113536 | tf_op jit(solution)/shard_map/jit(_take)/gather | solution.py:102
  298.7 198.1 %all-reduce.8.cloned.1.call-done = f32[32,64,128]{2,0,1:T(8,128)} async-done(((f32[32,64,128]{2,0,1:T(8,128)}), f32[32,64,128]{2,0,1:T(8,128)}) %all-reduce.8.cloned.1.call-update) | async-done | bytes 1048592 | tf_op jit(solution)/shard_map/psum | solution.py:104
  496.7 4.4 convolution_bitcast_fusion
  501.1 1.8 copy.18
  502.9 3.2 reshape.39
  506.1 3.4 copy.19
  509.4 4.7 copy.20
  514.1 0.0 all-reduce.10.cloned.1.call-update
  514.1 486.8 %all-reduce.10.cloned.1.call-done = f32[512,4,16,4]{2,3,1,0:T(4,128)} async-done(((f32[512,4,16,4]{2,3,1,0:T(4,128)}), f32[512,4,16,4]{2,3,1,0:T(4,128)}) %all-reduce.10.cloned.1.call-update) | async-done | bytes 524304
  1000.9 0.0 copy-done.5
  1000.9 1.3 fusion.8
  (5 shorter events, 0.0 us)
Async XLA Ops:
  6.5 280.0 %copy-start = (bf16[8192,128]{1,0:T(8,128)(2,1)S(1)}, bf16[8192,128]{1,0:T(8,128)(2,1)}, u32[]{:S(2)}) copy-start(bf16[8192,128]{1,0:T(8,128)(2,1)} %param.17) | copy-start | bytes 6291460
  6.5 104.3 %copy-start.1 = (bf16[128,1792]{1,0:T(8,128)(2,1)S(1)}, bf16[128,1792]{1,0:T(8,128)(2,1)}, u32[]{:S(2)}) copy-start(bf16[128,1792]{1,0:T(8,128)(2,1)} %param.12) | copy-start | bytes 1376260
  6.5 105.9 %copy-start.3 = (bf16[1792,128]{1,0:T(8,128)(2,1)S(1)}, bf16[1792,128]{1,0:T(8,128)(2,1)}, u32[]{:S(2)}) copy-start(bf16[1792,128]{1,0:T(8,128)(2,1)} %param.14) | copy-start | bytes 1376260
  6.5 181.3 %all-reduce.12.cloned.1.call-start = ((), (), s32[]{:S(2)}) async-start(), calls=%async_computation.2 | async-start | bytes 2293760 | tf_op jit(solution)/shard_map/psum | solution.py:49
  113.5 155.0 %all-reduce.14.cloned.1.call-start = ((), (), s32[]{:S(2)}) async-start(), calls=%async_computation.3 | async-start | bytes 2293760 | tf_op jit(solution)/shard_map/psum | solution.py:50
  187.9 308.9 %all-reduce.8.cloned.1.call-start = ((), (), s32[]{:S(2)}) async-start(), calls=%async_computation | async-start | bytes 2097152 | tf_op jit(solution)/shard_map/psum | solution.py:104
  269.8 16.6 %copy-start.4 = (s32[64,64]{1,0:T(8,128)S(1)}, s32[64,64]{1,0:T(8,128)}, u32[]{:S(2)}) copy-start(s32[64,64]{1,0:T(8,128)} %param.18) | copy-start | bytes 49156
  271.4 1.0 copy-start.2
  275.5 1.0 copy-start.2
  279.6 1.0 copy-start.2
  283.8 1.0 copy-start.2
  286.3 714.6 %all-reduce.10.cloned.1.call-start = ((), (), s32[]{:S(2)}) async-start(), calls=%async_computation.1 | async-start | bytes 8388608
  514.1 486.8 %copy-start.5 = (f32[16,4]{0,1:T(4,128)S(1)}, f32[16,4]{0,1:T(4,128)}, u32[]{:S(2)}) copy-start(f32[16,4]{0,1:T(4,128)} %param.19) | copy-start | bytes 772
Sparse Core Ops, SparseCore 0:
  113.6 74.1 all-reduce.11
  191.0 77.3 all-reduce.13
  286.5 210.2 all-reduce.7
  514.3 486.6 all-reduce.9
